TPU v7x, 32 devices: a whole 2x2x4 slice. The times are simulated.
32 devices in a mesh: space: 8 (over z, y), mode: 4 (over x, core).
Axes of the slice: x: 2, y: 2, z: 4, core: 2. Of those that a mesh axis runs over, the one named last changes fastest.
Arguments:
- velocity: float32 [3, 128, 512, 256], P(None, 'space', 'mode'), may hold values from -6 to 6
- basis: float32 [32, 786432], P('mode', 'space'), may hold values from -42 to 42
- levels: float32 [8], replicated, may hold values from 0.02 to 0.15
- profile_index: int32 [256], replicated, may hold values from 0 to 7
- advect: float32 [256], replicated, may hold values from 0 to 0.4
Outputs:
- modes: float32 [32, 786432], P('mode', 'space')
- sigma: float32 [32], replicated
Inputs may be any that keep to these rules, and one draw needn't show every extreme that they name: `profile_index`: each entry picks one of the 8 viscosity levels.
All inputs are finite; a program needn't handle non-finite values.
Results may differ from a plain program's by a relative error of at most 0.0055.
Values sent between devices are 32-bit elements; how exact they have to be, the bound alone decides.
A program may use at most 128 MiB of HBM per device.

v0:
```python
import math

import jax
import jax.numpy as jnp
import numpy as np
from jax import lax
from jax.sharding import PartitionSpec as P

STRIDE = 4
MODES = 32
SWEEPS = 2
ROWS_DEV = 24576


def extended(x, sides, width):
    for axis, dim in sides:
        size, length = (lax.axis_size(axis), x.shape[dim])
        up = [(i, (i + 1) % size) for i in range(size)]
        down = [(j, i) for i, j in up]
        last = lax.slice_in_dim(x, length - width, length, axis=dim)
        leading = lax.slice_in_dim(x, 0, width, axis=dim)
        before = lax.ppermute(last, axis, up)
        after = lax.ppermute(leading, axis, down)
        x = jnp.concatenate([before, x, after], axis=dim)
    return x


def profile(levels, profile_index):
    table = (
        profile_index[:, None] == jnp.arange(levels.shape[0], dtype=jnp.int32)[None, :]
    ).astype(jnp.float32)
    viscosity = jnp.sum(table * levels[None, :], axis=1)
    middle = 0.5 * (viscosity[:-1] + viscosity[1:])
    face_up = jnp.concatenate([middle, viscosity[-1:]])
    face_down = jnp.concatenate([viscosity[:1], middle])
    return (viscosity, face_down, face_up)


def advance(field, viscosity, face_down, face_up, advect):
    center = field[:, 1:-1, 1:-1, :]
    east = field[:, 2:, 1:-1, :]
    west = field[:, :-2, 1:-1, :]
    north = field[:, 1:-1, 2:, :]
    south = field[:, 1:-1, :-2, :]
    walled = jnp.pad(center, ((0, 0), (0, 0), (0, 0), (1, 1)))
    upward = walled[..., 2:]
    downward = walled[..., :-2]
    lateral = east + west + north + south - 4.0 * center
    vertical = face_up * (upward - center) - face_down * (center - downward)
    return center + viscosity * lateral + vertical - 0.5 * advect * (east - west)


def coarsen(field):
    components, x_cells, z_cells, y_cells = field.shape
    plane = z_cells * y_cells
    slabs = field.reshape(components * (x_cells // STRIDE), STRIDE * plane)
    along_x = slabs[:, 0:plane]
    for offset in range(1, STRIDE):
        along_x = along_x + slabs[:, offset * plane : (offset + 1) * plane]
    lines = along_x.reshape(
        components * (x_cells // STRIDE) * (z_cells // STRIDE), STRIDE * y_cells
    )
    along_z = lines[:, 0:y_cells]
    for offset in range(1, STRIDE):
        along_z = along_z + lines[:, offset * y_cells : (offset + 1) * y_cells]
    cell_ids = jnp.arange(y_cells, dtype=jnp.int32)[:, None] // STRIDE
    box_ids = jnp.arange(y_cells // STRIDE, dtype=jnp.int32)[None, :]
    summing = (cell_ids == box_ids).astype(jnp.float32)
    boxed = jnp.dot(
        along_z, summing, precision=lax.Precision.HIGHEST, preferred_element_type=jnp.float32
    )
    return (boxed / math.sqrt(STRIDE**3)).reshape(-1)


def with_faces(field):
    return extended(field, (("space", 1), ("mode", 2)), 1)


def round_order(count, turn):
    players = [0] + [1 + (i_pos - 1 + turn) % (count - 1) for i_pos in range(1, count)]
    leading = players[: count // 2]
    trailing = [players[count - 1 - k_pos] for k_pos in range(count // 2)]
    return np.array(leading + trailing)


def reorder_table(count, turn):
    current = round_order(count, turn)
    following = round_order(count, (turn + 1) % (count - 1))
    where_now = np.zeros(count, dtype=np.int64)
    where_now[current] = np.arange(count)
    table = np.zeros((count, count), dtype=np.float32)
    table[where_now[following], np.arange(count)] = 1.0
    return table


def jacobi_sweep(joined, tables):
    count = joined.shape[1]
    half = count // 2
    for turn in range(count - 1):
        col_lead = joined[:, :half]
        col_trail = joined[:, half:]
        rot_lead = col_lead[:count]
        rot_trail = col_trail[:count]
        norm_lead = jnp.sum(rot_lead * rot_lead, axis=0)
        norm_trail = jnp.sum(rot_trail * rot_trail, axis=0)
        inner = jnp.sum(rot_lead * rot_trail, axis=0)
        contrast = norm_trail - norm_lead
        orient = jnp.where(contrast >= 0.0, 1.0, -1.0)
        denominator = jnp.abs(contrast) + jnp.sqrt(contrast * contrast + 4.0 * inner * inner)
        positive = denominator > 0.0
        tangent = jnp.where(
            positive, 2.0 * inner * orient / jnp.where(positive, denominator, 1.0), 0.0
        )
        cosine = 1.0 / jnp.sqrt(1.0 + tangent * tangent)
        sine_part = cosine * tangent
        rotated_pairs = jnp.concatenate(
            [cosine * col_lead - sine_part * col_trail, sine_part * col_lead + cosine * col_trail],
            axis=1,
        )
        joined = jnp.dot(
            rotated_pairs,
            tables[turn],
            precision=lax.Precision.HIGHEST,
            preferred_element_type=jnp.float32,
        )
    return joined


def jacobi(upper):
    count = upper.shape[1]
    start_order = round_order(count, 0)
    back_order = np.zeros(count, dtype=np.int64)
    back_order[start_order] = np.arange(count)
    tables = [jnp.asarray(reorder_table(count, turn)) for turn in range(count - 1)]
    joined = jnp.concatenate([upper, jnp.eye(count, dtype=jnp.float32)], axis=0)[:, start_order]
    joined = lax.fori_loop(
        0, SWEEPS, lambda sweep_index, state: jacobi_sweep(state, tables), joined
    )
    joined = joined[:, back_order]
    return (joined[:count], joined[count:])


def row_products(matrix):
    return lax.dot_general(
        matrix,
        matrix,
        (((1,), (1,)), ((), ())),
        precision=lax.Precision.HIGHEST,
        preferred_element_type=jnp.float32,
    )


def per_device(velocity, basis, levels, profile_index, advect):
    viscosity, face_down, face_up = profile(levels, profile_index)
    first = advance(with_faces(velocity), viscosity, face_down, face_up, advect)
    second = advance(with_faces(first), viscosity, face_down, face_up, advect)
    snapshots = jnp.stack([coarsen(first), coarsen(second)])
    whole_basis, whole_snaps = (
        lax.all_gather(basis, "mode", axis=0, tiled=True),
        lax.all_gather(snapshots, "mode", axis=1, tiled=True),
    )
    own_basis = lax.dynamic_slice_in_dim(
        whole_basis, lax.axis_index("mode") * ROWS_DEV, ROWS_DEV, 1
    )
    own_rows = jnp.concatenate([snapshots, own_basis], axis=0)
    stack = jnp.concatenate([whole_snaps, whole_basis], axis=0)
    gram = row_products(own_rows)
    lower = jnp.linalg.cholesky(lax.psum(gram, ("space", "mode")))
    rotated, right_vecs = jacobi(lower.T)
    kept = rotated[:, :MODES]
    sigma = jnp.sqrt(jnp.sum(kept * kept, axis=0))
    panel_width = basis.shape[0]
    coefficients = lax.dynamic_slice_in_dim(
        right_vecs, lax.axis_index("mode") * panel_width, panel_width, 1
    )
    modes = jnp.dot(
        coefficients.T, stack, precision=lax.Precision.HIGHEST, preferred_element_type=jnp.float32
    )
    return (modes, sigma)


def solution(mesh):
    return jax.shard_map(
        per_device,
        mesh=mesh,
        in_specs=(P(None, "space", "mode", None), P("mode", "space"), P(), P(), P()),
        out_specs=(P("mode", "space"), P()),
        check_vma=False,
    )
```

profile of v0, /device:TPU:0, one launch (start us, length us, event | category | flops | bytes accessed | tf_op | source)
XLA Modules:
  0.0 259.3 jit_solution(15348478312905911423)
XLA Ops:
  8.4 3.0 %collective-permute-start.1 = (f32[3,1,128,256]{3,2,1,0:T(8,128)S(1)}, f32[3,1,128,256]{3,2,1,0:T(8,128)S(1)}, u32[]{:S(2)}, u32[]{:S(2)}) collective-permute-start(f32[3,1,128,256]{3,2,1,0:T(8,128)S(1)} %get-tuple-element.438), channel_id=1, source_target_pairs={{0,4},{4,8},{8,12},{12,16},{16,20},{20,24},{24,28},{28,0},{1,5},{5... | collective-permute-start | bytes 1179656 | tf_op jit(solution)/shard_map/ppermute | solution.py:22
  11.4 3.1 %collective-permute-start = (f32[3,1,128,256]{3,2,1,0:T(8,128)S(1)}, f32[3,1,128,256]{3,2,1,0:T(8,128)S(1)}, u32[]{:S(2)}, u32[]{:S(2)}) collective-permute-start(f32[3,1,128,256]{3,2,1,0:T(8,128)S(1)} %get-tuple-element.437), channel_id=1, source_target_pairs={{4,0},{8,4},{12,8},{16,12},{20,16},{24,20},{28,24},{0,28},{5,1},{9... | collective-permute-start | bytes 1179656 | tf_op jit(solution)/shard_map/ppermute | solution.py:23
  16.6 2.0 pad_maximum_fusion.17
  18.7 9.5 %collective-permute-done.1 = f32[3,1,128,256]{3,2,1,0:T(8,128)S(1)} collective-permute-done((f32[3,1,128,256]{3,2,1,0:T(8,128)S(1)}, f32[3,1,128,256]{3,2,1,0:T(8,128)S(1)}, u32[]{:S(2)}, u32[]{:S(2)}) %collective-permute-start.1) | collective-permute-done | bytes 393248 | tf_op jit(solution)/shard_map/ppermute | solution.py:22
  28.2 4.1 %constant_dynamic-update-slice_fusion.1 = f32[3,18,128,256]{3,2,1,0:T(8,128)S(1)} fusion(f32[3,18,128,256]{3,2,1,0:T(8,128)S(1)} %constant_dynamic-update-slice_fusion.2, f32[3,16,128,256]{3,2,1,0:T(8,128)} %param.44), kind=kLoop, calls=%fused_computation.1012 | loop fusion | bytes 12582912
  32.4 2.8 %copy-done.1 = f32[3,18,128,256]{3,2,1,0:T(8,128)} copy-done((f32[3,18,128,256]{3,2,1,0:T(8,128)}, f32[3,18,128,256]{3,2,1,0:T(8,128)S(1)}, u32[]{:S(2)}) %copy-start.1) | copy-done | bytes 7077912
  35.9 3.0 %collective-permute-done.2 = f32[3,18,1,256]{3,2,1,0:T(1,128)S(1)} collective-permute-done((f32[3,18,1,256]{3,2,1,0:T(1,128)S(1)}, f32[3,18,1,256]{3,2,1,0:T(1,128)S(1)}, u32[]{:S(2)}, u32[]{:S(2)}) %collective-permute-start.2) | collective-permute-done | bytes 55328 | tf_op jit(solution)/shard_map/ppermute | solution.py:23
  38.9 2.1 collective-permute-done.3
  41.0 19.0 %fusion.635 = f32[3,16,128,256]{3,2,1,0:T(8,128)S(1)} fusion(f32[3,16,128,256]{3,2,1,0:T(8,128)} %param.44, f32[3,18,128,256]{3,2,1,0:T(8,128)} %copy-done.1, f32[3,18,1,256]{3,2,1,0:T(1,128)S(1)} %collective-permute-done.3, f32[3,18,1,256]{3,2,1,0:T(1,128)S(1)} %collective-permute-done.2, f32[3,1,128,256]{3,2,1,0:T(8,128)S(1)} %collective-permute-done, ...), kind=kLoop, calls=%fused_computation.938 | loop fusion | flops 31457280 | bytes 20561920 | tf_op jit(solution)/shard_map/sub | solution.py:50
  60.0 2.7 %copy-done = f32[3,16,128,256]{3,2,1,0:T(8,128)} copy-done((f32[3,16,128,256]{3,2,1,0:T(8,128)}, f32[3,16,128,256]{3,2,1,0:T(8,128)S(1)}, u32[]{:S(2)}) %copy-start) | copy-done | bytes 6291480
  63.5 6.1 %reshape.1121 = f32[12,131072]{1,0:T(8,128)} reshape(f32[3,16,128,256]{3,2,1,0:T(8,128)} %copy-done) | data formatting | bytes 12582912 | tf_op jit(solution)/shard_map/reshape | solution.py:56
  69.6 5.4 %collective-permute-start.4 = (f32[3,1,128,256]{3,2,1,0:T(8,128)}, f32[3,1,128,256]{3,2,1,0:T(8,128)S(1)}, u32[]{:S(2)}, u32[]{:S(2)}) collective-permute-start(f32[3,1,128,256]{3,2,1,0:T(8,128)} %get-tuple-element.436), channel_id=1, source_target_pairs={{4,0},{8,4},{12,8},{16,12},{20,16},{24,20},{28,24},{0,28},{5,1},{9... | collective-permute-start | bytes 1179656 | tf_op jit(solution)/shard_map/ppermute | solution.py:23
  75.0 3.9 %slice_add_fusion.3 = f32[12,32768]{1,0:T(8,128)S(1)} fusion(f32[12,131072]{1,0:T(8,128)} %reshape.1121), kind=kLoop, calls=%fused_computation.979 | loop fusion | flops 1179648 | bytes 7864320 | tf_op jit(solution)/shard_map/add | solution.py:59
  80.2 9.6 %collective-permute-done.4 = f32[3,1,128,256]{3,2,1,0:T(8,128)S(1)} collective-permute-done((f32[3,1,128,256]{3,2,1,0:T(8,128)}, f32[3,1,128,256]{3,2,1,0:T(8,128)S(1)}, u32[]{:S(2)}, u32[]{:S(2)}) %collective-permute-start.4) | collective-permute-done | bytes 393248 | tf_op jit(solution)/shard_map/ppermute | solution.py:23
  95.9 22.2 %fusion.642 = f32[3,16,128,256]{3,2,1,0:T(8,128)} fusion(f32[3,16,128,256]{3,2,1,0:T(8,128)} %copy-done, f32[3,18,1,256]{3,2,1,0:T(1,128)S(1)} %collective-permute-done.7, f32[3,1,128,256]{3,2,1,0:T(8,128)S(1)} %collective-permute-done.4, f32[3,1,128,256]{3,2,1,0:T(8,128)S(1)} %collective-permute-done.5, f32[3,18,1,256]{3,2,1,0:T(1,128)S(1)} %collective-permute-done.6, ...), kind=kLoop, calls=%fused_computation.945 | loop fusion | flops 37748736 | bytes 13484032 | tf_op jit(solution)/shard_map/sub | solution.py:50
  118.0 6.1 %reshape.1123 = f32[12,131072]{1,0:T(8,128)} reshape(f32[3,16,128,256]{3,2,1,0:T(8,128)} %fusion.642) | data formatting | bytes 12582912 | tf_op jit(solution)/shard_map/reshape | solution.py:56
  124.2 3.9 %slice_add_fusion = f32[12,32768]{1,0:T(8,128)S(1)} fusion(f32[12,131072]{1,0:T(8,128)} %reshape.1123), kind=kLoop, calls=%fused_computation.976 | loop fusion | flops 1179648 | bytes 7864320 | tf_op jit(solution)/shard_map/add | solution.py:59
  131.6 8.5 %all_gather.7 = f32[2,98304]{1,0:T(2,128)S(1)} all-gather(f32[2,24576]{1,0:T(2,128)S(1)} %pad_maximum_fusion.12), channel_id=1, replica_groups=mesh['space'=8,'mode'=4] {'mode'}, dimensions={1}, use_global_device_ids=true | all-gather | bytes 983040 | tf_op jit(solution)/shard_map/all_gather | solution.py:160
  140.2 2.1 constant_dynamic-slice_fusion
  142.3 3.4 %fusion.655 = f32[34,34]{0,1:T(8,128)S(1)} fusion(f32[32,24576]{1,0:T(8,128)S(1)} %constant_dynamic-slice_fusion, f32[1,24576]{1,0:T(1,128)S(1)} %stack_reshape.7, f32[1,24576]{1,0:T(1,128)S(1)} %stack_reshape.6), kind=kOutput, calls=%fused_computation.970 | convolution fusion | flops 342589440 | bytes 3346960 | tf_op jit(solution)/shard_map/dot_general | solution.py:144
  145.8 39.8 %psum.7 = f32[34,34]{0,1:T(8,128)S(1)} all-reduce(f32[34,34]{0,1:T(8,128)S(1)} %fusion.655), channel_id=1, replica_groups=mesh['space'=8,'mode'=4] {'space','mode'}, use_global_device_ids=true, to_apply=%region_1.2 | all-reduce | flops 1156 | bytes 9248 | tf_op jit(solution)/shard_map/psum | solution.py:168
  185.7 3.1 %cholesky.20 = f32[34,34]{1,0:T(8,128)S(1)} custom-call(f32[34,34]{1,0:T(8,128)S(1)} %fusion.665), custom_call_target="Cholesky" | custom-call | tf_op jit(solution)/shard_map/jit(cholesky)/cholesky | solution.py:168
  190.9 47.8 %while.12 = (s32[]{:T(128)}, f32[68,34]{0,1:T(8,128)S(1)}, s32[]{:T(128)}, f32[17,34]{1,0:T(8,128)S(1)}, f32[17,34]{1,0:T(8,128)S(1)}) while((s32[]{:T(128)}, f32[68,34]{0,1:T(8,128)S(1)}, s32[]{:T(128)}, f32[17,34]{1,0:T(8,128)S(1)}, f32[17,34]{1,0:T(8,128)S(1)}) %tuple.274), condition=%wide.region_104.105_spmd.clone.clone, body=%wide.region_4.104_spmd.sunk.clone.clone.sunk | while | flops 31557920 | bytes 3961909 | solution.py:136
  240.1 12.4 %fusion.627 = f32[8,98304]{1,0:T(8,128)} fusion(f32[32,98304]{1,0:T(8,128)} %all-gather.2.cloned.1.call-done, f32[2,98304]{1,0:T(2,128)S(1)} %all_gather.7, f32[34,34]{0,1:T(8,128)S(1)} %slice.1260, s32[]{:T(128)S(6)} %select_n.1026), kind=kOutput, calls=%fused_computation.926 | convolution fusion | flops 324206592 | bytes 16519172 | tf_op jit(solution)/shard_map/dot_general | solution.py:176
  (381 shorter events, 65.8 us)
Async XLA Ops:
  7.2 133.0 %all-gather.2.cloned.1.call-start = ((), (), s32[]{:S(2)}) async-start(), calls=%async_computation | async-start | bytes 15728640 | tf_op jit(solution)/shard_map/all_gather | solution.py:159
  8.4 19.8 %collective-permute-start.1 = (f32[3,1,128,256]{3,2,1,0:T(8,128)S(1)}, f32[3,1,128,256]{3,2,1,0:T(8,128)S(1)}, u32[]{:S(2)}, u32[]{:S(2)}) collective-permute-start(f32[3,1,128,256]{3,2,1,0:T(8,128)S(1)} %get-tuple-element.438), channel_id=1, source_target_pairs={{0,4},{4,8},{8,12},{12,16},{16,20},{20,24},{24,28},{28,0},{1,5},{5... | collective-permute-start | bytes 1179656 | tf_op jit(solution)/shard_map/ppermute | solution.py:22
  11.4 21.0 %collective-permute-start = (f32[3,1,128,256]{3,2,1,0:T(8,128)S(1)}, f32[3,1,128,256]{3,2,1,0:T(8,128)S(1)}, u32[]{:S(2)}, u32[]{:S(2)}) collective-permute-start(f32[3,1,128,256]{3,2,1,0:T(8,128)S(1)} %get-tuple-element.437), channel_id=1, source_target_pairs={{4,0},{8,4},{12,8},{16,12},{20,16},{24,20},{28,24},{0,28},{5,1},{9... | collective-permute-start | bytes 1179656 | tf_op jit(solution)/shard_map/ppermute | solution.py:23
  32.4 2.8 %copy-start.1 = (f32[3,18,128,256]{3,2,1,0:T(8,128)}, f32[3,18,128,256]{3,2,1,0:T(8,128)S(1)}, u32[]{:S(2)}) copy-start(f32[3,18,128,256]{3,2,1,0:T(8,128)S(1)} %constant_dynamic-update-slice_fusion) | copy-start | bytes 21233668
  35.4 3.6 %collective-permute-start.2 = (f32[3,18,1,256]{3,2,1,0:T(1,128)S(1)}, f32[3,18,1,256]{3,2,1,0:T(1,128)S(1)}, u32[]{:S(2)}, u32[]{:S(2)}) collective-permute-start(f32[3,18,1,256]{3,2,1,0:T(1,128)S(1)} %get-tuple-element.433), channel_id=1, source_target_pairs={{1,0},{2,1},{3,2},{0,3},{5,4},{6,5},{7,6},{4,7},{9,8},{10,9},{11,1... | collective-permute-start | bytes 165896 | tf_op jit(solution)/shard_map/ppermute | solution.py:23
  35.8 5.2 %collective-permute-start.3 = (f32[3,18,1,256]{3,2,1,0:T(1,128)S(1)}, f32[3,18,1,256]{3,2,1,0:T(1,128)S(1)}, u32[]{:S(2)}, u32[]{:S(2)}) collective-permute-start(f32[3,18,1,256]{3,2,1,0:T(1,128)S(1)} %get-tuple-element.434), channel_id=1, source_target_pairs={{0,1},{1,2},{2,3},{3,0},{4,5},{5,6},{6,7},{7,4},{8,9},{9,10},{10,1... | collective-permute-start | bytes 165896 | tf_op jit(solution)/shard_map/ppermute | solution.py:22
  60.0 2.7 %copy-start = (f32[3,16,128,256]{3,2,1,0:T(8,128)}, f32[3,16,128,256]{3,2,1,0:T(8,128)S(1)}, u32[]{:S(2)}) copy-start(f32[3,16,128,256]{3,2,1,0:T(8,128)S(1)} %fusion.635) | copy-start | bytes 18874372
  69.6 20.2 %collective-permute-start.4 = (f32[3,1,128,256]{3,2,1,0:T(8,128)}, f32[3,1,128,256]{3,2,1,0:T(8,128)S(1)}, u32[]{:S(2)}, u32[]{:S(2)}) collective-permute-start(f32[3,1,128,256]{3,2,1,0:T(8,128)} %get-tuple-element.436), channel_id=1, source_target_pairs={{4,0},{8,4},{12,8},{16,12},{20,16},{24,20},{28,24},{0,28},{5,1},{9... | collective-permute-start | bytes 1179656 | tf_op jit(solution)/shard_map/ppermute | solution.py:23
  75.0 15.0 %collective-permute-start.5 = (f32[3,1,128,256]{3,2,1,0:T(8,128)S(1)}, f32[3,1,128,256]{3,2,1,0:T(8,128)S(1)}, u32[]{:S(2)}, u32[]{:S(2)}) collective-permute-start(f32[3,1,128,256]{3,2,1,0:T(8,128)S(1)} %get-tuple-element.435), channel_id=1, source_target_pairs={{0,4},{4,8},{8,12},{12,16},{16,20},{20,24},{24,28},{28,0},{1,5},{5... | collective-permute-start | bytes 1179656 | tf_op jit(solution)/shard_map/ppermute | solution.py:22
  91.2 2.7 %collective-permute-start.6 = (f32[3,18,1,256]{3,2,1,0:T(1,128)S(1)}, f32[3,18,1,256]{3,2,1,0:T(1,128)S(1)}, u32[]{:S(2)}, u32[]{:S(2)}) collective-permute-start(f32[3,18,1,256]{3,2,1,0:T(1,128)S(1)} %get-tuple-element.431), channel_id=1, source_target_pairs={{1,0},{2,1},{3,2},{0,3},{5,4},{6,5},{7,6},{4,7},{9,8},{10,9},{11,1... | collective-permute-start | bytes 165896 | tf_op jit(solution)/shard_map/ppermute | solution.py:23
  91.8 4.1 %collective-permute-start.7 = (f32[3,18,1,256]{3,2,1,0:T(1,128)S(1)}, f32[3,18,1,256]{3,2,1,0:T(1,128)S(1)}, u32[]{:S(2)}, u32[]{:S(2)}) collective-permute-start(f32[3,18,1,256]{3,2,1,0:T(1,128)S(1)} %get-tuple-element.432), channel_id=1, source_target_pairs={{0,1},{1,2},{2,3},{3,0},{4,5},{5,6},{6,7},{7,4},{8,9},{9,10},{10,1... | collective-permute-start | bytes 165896 | tf_op jit(solution)/shard_map/ppermute | solution.py:22
  140.2 50.8 %copy-start.2 = (f32[17,34]{1,0:T(8,128)S(1)}, f32[17,34]{1,0:T(8,128)}, u32[]{:S(2)}) copy-start(f32[17,34]{1,0:T(8,128)} %constant.990) | copy-start | bytes 6940
  140.2 50.8 %copy-start.3 = (f32[17,34]{1,0:T(8,128)S(1)}, f32[17,34]{1,0:T(8,128)}, u32[]{:S(2)}) copy-start(f32[17,34]{1,0:T(8,128)} %constant.991) | copy-start | bytes 6940
Sparse Core Ops, SparseCore 0:
  14.7 82.3 all-gather.1
where the time goes:
time: 260 us; the launch traced here: 259 us
  other arithmetic  70.4 us (27%)
  matrix products  53.9 us (21%)
  blocking collectives  48.3 us (19%)
  local copies, waits for them, and re-layouts  32 us (12%)
  waiting for transfers between devices  26.4 us (10%)
  between operations  14.2 us (5%)
  starting transfers between devices  12.7 us (5%)
    sub x2, other arithmetic, advance(): center + viscosity * lateral + vertical - 0.5 * advect * (east - west)  41.2 us
    psum x1, blocking collectives, per_device(): lower = jnp.linalg.cholesky(lax.psum(gram, ('space', 'mode')))  39.8 us
    dot_general x132, matrix products, jacobi_sweep(): jnp.dot(rotated_pairs, tables[turn], precision=lax.Precision.HIGHEST, pre...  34.5 us
    ppermute x4, waiting for transfers between devices, extended(): before = lax.ppermute(last, axis, up)  13.7 us
    ppermute x4, waiting for transfers between devices, extended(): after = lax.ppermute(leading, axis, down)  12.6 us
    dot_general x1, matrix products, per_device(): jnp.dot(coefficients.T, stack, precision=lax.Precision.HIGHEST, preferred...  12.4 us
    reshape x2, local copies, waits for them, and re-layouts, coarsen(): slabs = field.reshape(components * (x_cells // STRIDE), STRIDE * plane)  12.3 us
    reduce_sum x66, other arithmetic, jacobi_sweep(): norm_lead = jnp.sum(rot_lead * rot_lead, axis=0)  10.1 us
  transfers between devices with their start and end apart: 9, of which 6 were waited for; matrix products, arithmetic and copies ran while one was open for 30% of the time, Pallas kernels for 0%

commit v1 on v0

v1 whole, which is shorter than its diff:
```python
import functools
import math

import jax
import jax.numpy as jnp
import numpy as np
from jax import lax
from jax.experimental import pallas as pl
from jax.experimental.pallas import tpu as pltpu
from jax.sharding import PartitionSpec as P

STRIDE = 4
MODES = 32
SWEEPS = 2
COUNT = MODES + 2
HALF = COUNT // 2
ZB = 48
F32 = jnp.float32
BF16 = jnp.bfloat16
HIGH = lax.Precision.HIGHEST


def box_taps():
    lap = np.array([1.0, -2.0, 1.0])
    grad = np.array([-1.0, 0.0, 1.0])
    fixed = []
    for ops in ([], [lap], [grad], [lap, lap], [lap, grad], [grad, grad]):
        taps = np.zeros(STRIDE + 4)
        for x in range(STRIDE):
            terms = {x + 2: 1.0}
            for op in ops:
                nxt = {}
                for pos, val in terms.items():
                    for off, w in zip((-1, 0, 1), op):
                        if w:
                            nxt[pos + off] = nxt.get(pos + off, 0.0) + val * w
                terms = nxt
            for pos, val in terms.items():
                taps[pos] += val
        fixed.append(taps)
    return fixed


def z_table(cz):
    taps = box_taps()
    boxes = cz // STRIDE
    order = list(range(0, boxes, 2)) + list(range(1, boxes, 2)) + [-1, boxes]
    table = np.zeros((3 * ZB, 2 * cz), np.float32)
    for block, which in enumerate((0, 1, 3)):
        for row, box in enumerate(order):
            for k in range(STRIDE + 4):
                z = box * STRIDE - 2 + k
                if 0 <= z < cz:
                    table[block * ZB + row, z] = taps[which][k]
                    table[block * ZB + row, cz + z] = taps[which][k]
    return table


def column(row, width):
    size = row.shape[1]
    eye = lax.broadcasted_iota(jnp.int32, (size, size), 0) == lax.broadcasted_iota(
        jnp.int32, (size, size), 1
    )
    diag = jnp.where(eye, jnp.broadcast_to(row, (size, size)), 0.0)
    return jnp.dot(diag, jnp.ones((size, width), F32), precision=HIGH, preferred_element_type=F32)


def split(x):
    high = x.astype(BF16)
    return high, (x - high.astype(F32)).astype(BF16)


def wall_tables(levels_ref, index_ref, advect_ref, yh_ref, yl_ref):
    ny = index_ref.shape[1]
    nb = ny // STRIDE
    width = 2 * nb
    index = index_ref[...]
    nu_row = jnp.zeros((1, ny), F32)
    for level in range(levels_ref.shape[0]):
        nu_row = jnp.where(index == level, levels_ref[level], nu_row)
    nu = column(nu_row, width)
    adv = 0.5 * column(advect_ref[...], width)
    rows = lax.broadcasted_iota(jnp.int32, (ny, width), 0)
    lanes = lax.broadcasted_iota(jnp.int32, (ny, width), 1)
    below = lambda x: pltpu.roll(x, 1, 0)
    above = lambda x: pltpu.roll(x, ny - 1, 0)
    up = jnp.where(rows == ny - 1, nu, 0.5 * (nu + above(nu)))
    down = jnp.where(rows == 0, nu, 0.5 * (below(nu) + nu))
    main = 1.0 - up - down
    from_below = jnp.where(rows == 0, 0.0, below(up))
    from_above = jnp.where(rows == ny - 1, 0.0, above(down))

    def wall(x):
        return main * x + from_below * below(x) + from_above * above(x)

    box = jnp.where(lanes < nb, lanes, lanes - nb)
    x = jnp.where(rows // STRIDE == box, 1.0 / math.sqrt(STRIDE**3), 0.0)
    one = lanes < nb
    mx = wall(x)
    parts = [
        jnp.where(one, mx, wall(mx)),
        jnp.where(one, nu * x, nu * mx + wall(nu * x)),
        -jnp.where(one, adv * x, adv * mx + wall(adv * x)),
        jnp.where(one, 0.0, nu * nu * x),
        jnp.where(one, 0.0, -2.0 * nu * adv * x),
        jnp.where(one, 0.0, adv * adv * x),
    ]
    for k, part in enumerate(parts):
        high, low = split(part)
        yh_ref[k * ny : (k + 1) * ny, :] = high
        yl_ref[k * ny : (k + 1) * ny, :] = low


def coarse_box(v_ref, z_ref, yh_ref, yl_ref, f_ref, u_ref, c, jj):
    cx, cz, ny = v_ref.shape[1:]
    taps = box_taps()
    start = (jj - 1) * STRIDE - 2
    zc = 16

    def body(i, carry):
        at = pl.multiple_of(i * zc, zc)
        slabs = {
            k: v_ref[c, start + k, pl.ds(at, zc), :]
            for k in range(STRIDE + 4)
            if 0 <= start + k < cx
        }
        for f, coefs in enumerate(taps):
            total = None
            groups = {}
            for k, slab in slabs.items():
                if coefs[k]:
                    groups.setdefault(abs(coefs[k]), []).append((coefs[k] > 0, slab))
            for size, members in groups.items():
                part = None
                for plus, slab in sorted(members, key=lambda m: not m[0]):
                    if part is None:
                        part = slab if plus else -slab
                    else:
                        part = part + slab if plus else part - slab
                part = part if size == 1 else part * size
                total = part if total is None else total + part
            if total is None:
                total = jnp.zeros((zc, ny), F32)
            high, low = split(total)
            f_ref[pl.ds(at, zc), f * ny : (f + 1) * ny] = high
            f_ref[pl.ds(pl.multiple_of(cz + at, zc), zc), f * ny : (f + 1) * ny] = low
        return carry

    lax.fori_loop(0, cz // zc, body, 0)
    z0 = z_ref[0:ZB, :]

    def along_z(z, f):
        return jnp.dot(z, f_ref[:, f * ny : (f + 1) * ny], preferred_element_type=F32)

    z012_f0 = along_z(z_ref[...], 0)
    z01_f1 = along_z(z_ref[0 : 2 * ZB, :], 1)
    z01_f2 = along_z(z_ref[0 : 2 * ZB, :], 2)
    fields = [
        z012_f0[0:ZB],
        z01_f1[0:ZB] + z012_f0[ZB : 2 * ZB],
        z01_f2[0:ZB],
        along_z(z0, 3) + 2.0 * z01_f1[ZB : 2 * ZB] + z012_f0[2 * ZB : 3 * ZB],
        along_z(z0, 4) + z01_f2[ZB : 2 * ZB],
        along_z(z0, 5),
    ]
    out = None
    for k, field in enumerate(fields):
        high, low = split(field)
        yh = yh_ref[k * ny : (k + 1) * ny, :]
        yl = yl_ref[k * ny : (k + 1) * ny, :]
        both = jnp.dot(jnp.concatenate([high, low], axis=0), yh, preferred_element_type=F32)
        term = both[:ZB] + both[ZB:] + jnp.dot(high, yl, preferred_element_type=F32)
        out = term if out is None else out + term
    u_ref[jj, c, :, :] = out


def placed(rows, trail):
    row = lax.broadcasted_iota(jnp.int32, (rows, 128), 0)
    lane = lax.broadcasted_iota(jnp.int32, (rows, 128), 1)
    player = COUNT - 1 - lane if trail else lane
    where = jnp.where(player < 2, player, player + 6)
    return jnp.where((lane < HALF) & (row == where), 1.0, 0.0).astype(F32)


def jacobi(gram):
    rows = gram.shape[0]
    lead_v, trail_v = placed(rows, False), placed(rows, True)
    square = gram[:, :rows]
    lead_w = jnp.dot(square, lead_v, precision=HIGH, preferred_element_type=F32)
    trail_w = jnp.dot(square, trail_v, precision=HIGH, preferred_element_type=F32)
    lane = lax.broadcasted_iota(jnp.int32, (rows, 128), 1)
    first, last = lane == 0, lane == HALF - 1

    def turn(_, state):
        lw, lv, tw, tv = state
        a = jnp.sum(lw * lv, axis=0, keepdims=True)
        b = jnp.sum(tw * tv, axis=0, keepdims=True)
        c = jnp.sum(lv * tw, axis=0, keepdims=True)
        contrast = b - a
        orient = jnp.where(contrast >= 0.0, 2.0, -2.0)
        denominator = jnp.abs(contrast) + jnp.sqrt(contrast * contrast + 4.0 * c * c)
        positive = denominator > 0.0
        tangent = jnp.where(positive, c * orient / jnp.where(positive, denominator, 1.0), 0.0)
        cosine = lax.rsqrt(1.0 + tangent * tangent)
        sine = cosine * tangent

        def move(lead, trail):
            new_lead = cosine * lead - sine * trail
            new_trail = sine * lead + cosine * trail
            shifted = pltpu.roll(new_lead, 127, 1)
            next_lead = jnp.where(first, new_lead, jnp.where(last, new_trail, shifted))
            next_trail = jnp.where(first, shifted, pltpu.roll(new_trail, 1, 1))
            return next_lead, next_trail

        lw, tw = move(lw, tw)
        lv, tv = move(lv, tv)
        return lw, lv, tw, tv

    lw, lv, tw, tv = lax.fori_loop(
        0, SWEEPS * (COUNT - 1), turn, (lead_w, lead_v, trail_w, trail_v)
    )
    norm_lead = jnp.sum(lw * lv, axis=0, keepdims=True)
    norm_trail = jnp.sum(tw * tv, axis=0, keepdims=True)
    return lv, tv, norm_lead, norm_trail


def kernel(
    n_space, n_mode,
    velocity_ref, basis_ref, levels_ref, index_ref, advect_ref, z_ref,
    out_ref, sigma_ref,
    v_ref, stack_ref, yh_ref, yl_ref, f_ref, u_ref, xr_ref, zs_ref, zr_ref, sn_ref, row_ref,
    gram_ref, gm_ref, gs_ref,
    v_sem, own_sem,
    s1_send, s1_recv, mate_send, mate_recv, s2_send, s2_recv, fb_send, fb_recv, fa_send, fa_recv,
    x_send, x_recv, z_send, z_recv, sn_send, sn_recv, gm_send, gm_recv, gs_send, gs_recv,
):
    space, mode = lax.axis_index("space"), lax.axis_index("mode")
    mb, cols = basis_ref.shape
    quarter = cols // n_mode
    components, cx, cz, ny = velocity_ref.shape
    nxb, nzb, nb = cx // STRIDE, cz // STRIDE, ny // STRIDE
    pairs = n_mode // 2
    pair, side = mode // 2, mode % 2
    mate = pair * 2 + 1 - side
    MESH = pl.DeviceIdType.MESH

    def mode_peer(o):
        return lax.rem(mode + o, n_mode)

    def space_peer(o):
        return lax.rem(space + o, n_space)

    def rows_of(m):
        return pl.ds(pl.multiple_of(m * mb, mb), mb)

    def cols_of(q, count=1):
        return pl.ds(pl.multiple_of(q * quarter, quarter), count * quarter)

    def remote(src, dst, send, recv, s, m):
        return pltpu.make_async_remote_copy(
            src_ref=src, dst_ref=dst, send_sem=send, recv_sem=recv,
            device_id=(s, m), device_id_type=MESH,
        )

    v_copies = []
    for c in range(components):
        copy = pltpu.make_async_copy(velocity_ref.at[c], v_ref.at[c], v_sem.at[c])
        copy.start()
        v_copies.append(copy)
    own = pltpu.make_async_copy(basis_ref, stack_ref.at[rows_of(mode)], own_sem)
    own.start()

    barrier = pltpu.get_barrier_semaphore()
    for o in range(1, n_mode):
        pl.semaphore_signal(barrier, inc=1, device_id=(space, mode_peer(o)), device_id_type=MESH)
    for o in range(1, n_space):
        pl.semaphore_signal(barrier, inc=1, device_id=(space_peer(o), mode), device_id_type=MESH)
    pl.semaphore_wait(barrier, n_mode - 1 + n_space - 1)

    stage1 = []
    for o in range(1, n_mode):
        peer = mode_peer(o)
        copy = remote(
            basis_ref.at[:, cols_of(peer)], stack_ref.at[rows_of(mode), cols_of(peer)],
            s1_send.at[o - 1], s1_recv.at[o - 1], space, peer,
        )
        copy.start()
        stage1.append(copy)
    mates = []
    mate_cols = [cols_of(mode)] + [
        cols_of(2 * lax.rem(pair + g, pairs), 2) for g in range(1, pairs)
    ]
    for i, where in enumerate(mate_cols):
        copy = remote(
            basis_ref.at[:, where], stack_ref.at[rows_of(mode), where],
            mate_send.at[i], mate_recv.at[i], space, mate,
        )
        copy.start()
        mates.append(copy)

    wall_tables(levels_ref, index_ref, advect_ref, yh_ref, yl_ref)
    row_ref[...] = jnp.zeros_like(row_ref)
    zs_ref[...] = jnp.zeros_like(zs_ref)
    for copy in v_copies:
        copy.wait()

    def boxes(jj):
        def body(c, carry):
            coarse_box(v_ref, z_ref, yh_ref, yl_ref, f_ref, u_ref, c, jj)
            return carry

        lax.fori_loop(0, components, body, 0)

    boxes(0)
    boxes(nxb + 1)
    x_copies = [
        remote(u_ref.at[0], xr_ref.at[0], x_send.at[0], x_recv.at[0], space_peer(n_space - 1), mode),
        remote(u_ref.at[nxb + 1], xr_ref.at[1], x_send.at[1], x_recv.at[1], space_peer(1), mode),
    ]
    for copy in x_copies:
        copy.start()
    for jj in range(1, nxb + 1):
        boxes(jj)
    for copy in x_copies:
        copy.wait()
    for c in range(components):
        u_ref[nxb, c, :, :] = u_ref[nxb, c, :, :] + xr_ref[0, c, :, :]
        u_ref[1, c, :, :] = u_ref[1, c, :, :] + xr_ref[1, c, :, :]
    for c in range(components):
        for jj in range(1, nxb + 1):
            row = c * nxb + jj - 1
            for d in range(2):
                zs_ref[d, row : row + 1, :] = u_ref[jj, c, nzb + d : nzb + d + 1, :]
    z_copies = [
        remote(zs_ref.at[0], zr_ref.at[0], z_send.at[0], z_recv.at[0], space, mode_peer(n_mode - 1)),
        remote(zs_ref.at[1], zr_ref.at[1], z_send.at[1], z_recv.at[1], space, mode_peer(1)),
    ]
    for copy in z_copies:
        copy.start()
    for copy in z_copies:
        copy.wait()
    half = nzb // 2
    lanes = lax.broadcasted_iota(jnp.int32, (half, 2 * nb), 1) < nb
    for c in range(components):
        for jj in range(1, nxb + 1):
            row = c * nxb + jj - 1
            u_ref[jj, c, nzb - 1 : nzb, :] = u_ref[jj, c, nzb - 1 : nzb, :] + zr_ref[0, row : row + 1, :]
            u_ref[jj, c, 0:1, :] = u_ref[jj, c, 0:1, :] + zr_ref[1, row : row + 1, :]
            even = u_ref[jj, c, 0:half, :]
            odd = u_ref[jj, c, half:nzb, :]
            one = jnp.where(lanes, even, pltpu.roll(odd, nb, 1))
            two = jnp.where(lanes, pltpu.roll(even, nb, 1), odd)
            at = row * half
            sn_ref[mode, 0, at : at + half, :] = one
            sn_ref[mode, 1, at : at + half, :] = two
            for k in range(half):
                lane_at = (at + k) * 2 * nb
                row_ref[0:1, lane_at : lane_at + 2 * nb] = one[k : k + 1]
                row_ref[1:2, lane_at : lane_at + 2 * nb] = two[k : k + 1]
    sn_copies = []
    for o in range(1, n_mode):
        copy = remote(
            sn_ref.at[mode], sn_ref.at[mode], sn_send.at[o - 1], sn_recv.at[o - 1],
            space, mode_peer(o),
        )
        copy.start()
        sn_copies.append(copy)

    for copy in stage1:
        copy.wait()
    own.wait()
    forward_b = []
    for g in range(1, pairs):
        theirs = pl.ds(pl.multiple_of(2 * mb * lax.rem(pair + g, pairs), 2 * mb), 2 * mb)
        where = stack_ref.at[theirs, cols_of(mode)]
        copy = remote(where, where, fb_send.at[g - 1], fb_recv.at[g - 1], space, mate)
        copy.start()
        forward_b.append(copy)
    stage2 = []
    for g in range(1, pairs):
        for k in range(1, pairs):
            there = lax.rem(pair + g, pairs)
            piece = lax.rem(there + k, pairs)
            for part in range(2):
                i = ((g - 1) * (pairs - 1) + k - 1) * 2 + part
                where = cols_of(2 * piece + part)
                copy = remote(
                    basis_ref.at[:, where], stack_ref.at[rows_of(mode), where],
                    s2_send.at[i], s2_recv.at[i], space, 2 * there + side,
                )
                copy.start()
                source = lax.rem(pair - g + pairs, pairs)
                here = lax.rem(pair + k, pairs)
                stage2.append((copy, i, source, 2 * here + part))

    kc = 2048

    def gram_body(i, carry):
        at = pl.multiple_of(i * kc, kc)
        wide = pl.multiple_of(mode * quarter + i * kc, kc)
        x = jnp.concatenate([row_ref[:, pl.ds(at, kc)], stack_ref[:, pl.ds(wide, kc)]], axis=0)
        high, low = split(x)
        both = jnp.concatenate([high, low], axis=0)
        return carry + lax.dot_general(
            both, high, (((1,), (1,)), ((), ())), preferred_element_type=F32
        )

    size = 16 + stack_ref.shape[0]
    gram2 = lax.fori_loop(0, quarter // kc, gram_body, jnp.zeros((2 * size, size), F32))
    cross = gram2[size:]
    gram = gram2[:size] + cross + cross.T
    gram = jnp.concatenate([gram[0:8], gram[16:]], axis=0)
    gram = jnp.concatenate([gram[:, 0:8], gram[:, 16:], jnp.zeros((size - 8, 128 - size + 8), F32)], axis=1)
    gm_ref[mode, :, :] = gram
    gm_copies = []
    for o in range(1, n_mode):
        copy = remote(
            gm_ref.at[mode], gm_ref.at[mode], gm_send.at[o - 1], gm_recv.at[o - 1],
            space, mode_peer(o),
        )
        copy.start()
        gm_copies.append(copy)
    for copy in gm_copies:
        copy.wait()
    total = gm_ref[0]
    for m in range(1, n_mode):
        total = total + gm_ref[m]
    gs_ref[space, :, :] = total
    gs_copies = []
    for o in range(1, n_space):
        copy = remote(
            gs_ref.at[space], gs_ref.at[space], gs_send.at[o - 1], gs_recv.at[o - 1],
            space_peer(o), mode,
        )
        copy.start()
        gs_copies.append(copy)
    for copy in gs_copies:
        copy.wait()
    total = gs_ref[0]
    for s in range(1, n_space):
        total = total + gs_ref[s]

    lead, trail, norm_lead, norm_trail = jacobi(total)

    def pick(first, count, lead_side):
        row = lax.broadcasted_iota(jnp.int32, (count, 128), 0) + first
        lane = lax.broadcasted_iota(jnp.int32, (count, 128), 1)
        player = lane if lead_side else COUNT - 1 - lane
        return jnp.where((lane < HALF) & (row == player), 1.0, 0.0).astype(F32)

    def across(a, b):
        return lax.dot_general(
            a, b, (((1,), (1,)), ((), ())), precision=HIGH, preferred_element_type=F32
        )

    norms = across(jnp.broadcast_to(norm_lead, (8, 128)), pick(0, 128, True)) + across(
        jnp.broadcast_to(norm_trail, (8, 128)), pick(0, 128, False)
    )
    sigma_ref[...] = jnp.sqrt(norms)
    sel_lead, sel_trail = pick(mode * mb, mb, True), pick(mode * mb, mb, False)
    lead_b = jnp.concatenate([lead[8:], lead[8:]], axis=0)
    trail_b = jnp.concatenate([trail[8:], trail[8:]], axis=0)
    coef = across(sel_lead, lead_b) + across(sel_trail, trail_b)
    coef_high = coef.astype(BF16).astype(F32)
    left = jnp.concatenate([coef_high, coef - coef_high], axis=0).astype(BF16)
    snap = across(sel_lead, lead[0:8]) + across(sel_trail, trail[0:8])
    c0 = jnp.broadcast_to(snap[:, 0:1], (mb, 128))
    c1 = jnp.broadcast_to(snap[:, 1:2], (mb, 128))

    def emit(q):
        def body(i, carry):
            at = pl.multiple_of(q * quarter + i * kc, kc)
            high, low = split(stack_ref[:, pl.ds(at, kc)])
            both = jnp.concatenate([high, low], axis=0)
            done = jnp.dot(left, both, preferred_element_type=F32)
            done = done[:mb] + done[mb:]
            for t in range(kc // 128):
                r = i * (kc // 128) + t
                out_ref[:, pl.ds(pl.multiple_of(at + t * 128, 128), 128)] = (
                    done[:, t * 128 : (t + 1) * 128]
                    + c0 * sn_ref[q, 0, pl.ds(r, 1), :]
                    + c1 * sn_ref[q, 1, pl.ds(r, 1), :]
                )
            return carry

        lax.fori_loop(0, quarter // kc, body, 0)

    for copy in sn_copies + mates + forward_b:
        copy.wait()
    forward_a = []
    emit(2 * pair)
    for n, (copy, i, source, q) in enumerate(stage2):
        copy.wait()
        where = stack_ref.at[rows_of(2 * source + side), cols_of(q)]
        forward = remote(where, where, fa_send.at[i], fa_recv.at[i], space, mate)
        forward.start()
        forward_a.append(forward)
        if n == 0:
            emit(2 * pair + 1)
    if not stage2:
        emit(2 * pair + 1)
    for copy in forward_a:
        copy.wait()
    for o in range(2, n_mode):
        emit(lax.rem(2 * pair + o, n_mode))


def per_device(n_space, n_mode, velocity, basis, levels, profile_index, advect):
    components, cx, cz, ny = velocity.shape
    mb, cols = basis.shape
    quarter = cols // n_mode
    nxb, nzb, nb = cx // STRIDE, cz // STRIDE, ny // STRIDE
    pairs = n_mode // 2
    pieces = max(1, 2 * (pairs - 1) ** 2)
    dma = pltpu.SemaphoreType.DMA
    modes, sigma = pl.pallas_call(
        functools.partial(kernel, n_space, n_mode),
        out_shape=(
            jax.ShapeDtypeStruct((mb, cols), F32),
            jax.ShapeDtypeStruct((8, 128), F32),
        ),
        in_specs=[
            pl.BlockSpec(memory_space=pl.ANY),
            pl.BlockSpec(memory_space=pl.ANY),
            pl.BlockSpec(memory_space=pltpu.SMEM),
            pl.BlockSpec(memory_space=pltpu.VMEM),
            pl.BlockSpec(memory_space=pltpu.VMEM),
            pl.BlockSpec(memory_space=pltpu.VMEM),
        ],
        out_specs=(
            pl.BlockSpec(memory_space=pltpu.VMEM),
            pl.BlockSpec(memory_space=pltpu.VMEM),
        ),
        scratch_shapes=[
            pltpu.VMEM((components, cx, cz, ny), F32),
            pltpu.VMEM((n_mode * mb, cols), F32),
            pltpu.VMEM((6 * ny, 2 * nb), BF16),
            pltpu.VMEM((6 * ny, 2 * nb), BF16),
            pltpu.VMEM((2 * cz, 6 * ny), BF16),
            pltpu.VMEM((nxb + 2, components, ZB, 2 * nb), F32),
            pltpu.VMEM((2, components, ZB, 2 * nb), F32),
            pltpu.VMEM((2, 16, 2 * nb), F32),
            pltpu.VMEM((2, 16, 2 * nb), F32),
            pltpu.VMEM((n_mode, 2, components * nxb * nzb // 2, 2 * nb), F32),
            pltpu.VMEM((16, quarter), F32),
            pltpu.VMEM((8, 128), F32),
            pltpu.VMEM((n_mode, 8 + n_mode * mb, 128), F32),
            pltpu.VMEM((n_space, 8 + n_mode * mb, 128), F32),
            dma((components,)), dma,
            dma((n_mode - 1,)), dma((n_mode - 1,)),
            dma((pairs,)), dma((pairs,)),
            dma((pieces,)), dma((pieces,)),
            dma((max(1, pairs - 1),)), dma((max(1, pairs - 1),)),
            dma((pieces,)), dma((pieces,)),
            dma((2,)), dma((2,)),
            dma((2,)), dma((2,)),
            dma((n_mode - 1,)), dma((n_mode - 1,)),
            dma((n_mode - 1,)), dma((n_mode - 1,)),
            dma((n_space - 1,)), dma((n_space - 1,)),
        ],
        compiler_params=pltpu.CompilerParams(
            collective_id=0, has_side_effects=True, vmem_limit_bytes=56 * 1024 * 1024
        ),
    )(
        velocity,
        basis,
        levels,
        profile_index.reshape(1, -1),
        advect.reshape(1, -1),
        jnp.asarray(z_table(cz), BF16),
    )
    return modes, sigma[0, :MODES]


def solution(mesh):
    n_space, n_mode = mesh.shape["space"], mesh.shape["mode"]
    return jax.shard_map(
        functools.partial(per_device, n_space, n_mode),
        mesh=mesh,
        in_specs=(P(None, "space", "mode", None), P("mode", "space"), P(), P(), P()),
        out_specs=(P("mode", "space"), P()),
        check_vma=False,
    )
```

time: 260 us -> 119 us (0.46)
  Pallas kernels: 0 us -> 113 us
  other arithmetic: 70.4 us -> 0 us
  matrix products: 53.9 us -> 0 us
  blocking collectives: 48.3 us -> 0 us
  local copies, waits for them, and re-layouts: 32 us -> 4.94 us
  waiting for transfers between devices: 26.4 us -> 0 us
  between operations: 14.2 us -> 0.64 us
  starting transfers between devices: 12.7 us -> 0 us
    pallas_call x0 -> x1, Pallas kernels: none -> 113 us  [per_device(): pl.pallas_call(functools.partial(kernel, n_space, n_mode), out_shape=(jax...]
    dot_general x136 -> x0, matrix products: 53.9 us -> none  [the longest x132 34.5 us: jacobi_sweep(): jnp.dot(rotated_pairs, tables[turn], precision=lax.Precision.HIGHEST, pre...]
    sub x2 -> x0, other arithmetic: 41.2 us -> none  [advance(): center + viscosity * lateral + vertical - 0.5 * advect * (east - west)]
    psum x1 -> x0, blocking collectives: 39.8 us -> none  [per_device(): lower = jnp.linalg.cholesky(lax.psum(gram, ('space', 'mode')))]
    ppermute x8 -> x0, waiting for transfers between devices: 26.4 us -> none  [the longest x4 13.7 us: extended(): before = lax.ppermute(last, axis, up)]
    reshape x4 -> x0, local copies, waits for them, and re-layouts: 15 us -> none  [the longest x2 12.3 us: coarsen(): slabs = field.reshape(components * (x_cells // STRIDE), STRIDE * plane)]
    ppermute x8 -> x0, starting transfers between devices: 12.7 us -> none  [the longest x4 9.48 us: extended(): after = lax.ppermute(leading, axis, down)]
    reduce_sum x68 -> x0, other arithmetic: 11 us -> none  [the longest x66 10.1 us: jacobi_sweep(): norm_lead = jnp.sum(rot_lead * rot_lead, axis=0)]
  transfers between devices with their start and end apart: 9 -> 0, of which waited for: 6 -> 0; matrix products, arithmetic and copies ran while one was open for 30% -> 0% of each run, Pallas kernels for 0% -> 0%
where the time goes in v1:
time: 119 us; the launch traced here: 118 us
  Pallas kernels  113 us (95%)
  local copies, waits for them, and re-layouts  4.94 us (4%)
    pallas_call x1, Pallas kernels, per_device(): pl.pallas_call(functools.partial(kernel, n_space, n_mode), out_shape=(jax...  113 us
    unnamed x1, local copies, waits for them, and re-layouts  3.75 us

profile of v1, /device:TPU:0, one launch (start us, length us, event | category | flops | bytes accessed | tf_op | source)
XLA Modules:
  0.0 118.3 jit_solution(1125815582788863158)
XLA Ops:
  0.6 112.7 %shard_map.77 = (f32[8,98304]{1,0:T(8,128)}, f32[8,128]{1,0:T(8,128)}) custom-call(f32[3,16,128,256]{3,2,1,0:T(8,128)} %velocity_ref.1, f32[8,98304]{1,0:T(8,128)} %basis_ref.1, f32[8]{0:T(128)} %levels_ref.1, s32[1,256]{1,0:T(1,128)} %bitcast.4, f32[1,256]{1,0:T(1,128)} %bitcast.5, bf16[144,256]{1,0:T(8,128)(2,1)} %constant.2.clone.z_ref), custom_call_target="tpu_custom_call" | custom-call | tf_op jit(solution)/shard_map/pallas_call | solution.py:516
  113.3 1.2 %slice_bitcast_fusion = f32[32]{0:T(128)} fusion(f32[8,128]{1,0:T(8,128)} %get-tuple-element.5), kind=kLoop, calls=%fused_computation | loop fusion | bytes 256 | tf_op jit(solution)/shard_map/squeeze | solution.py:572
  114.5 3.8 %copy.9 = f32[8,98304]{1,0:T(8,128)} copy(f32[8,98304]{1,0:T(8,128)} %get-tuple-element.8) | data formatting | bytes 6291456

commit v2 on v1

--- a/solution.py
+++ b/solution.py
@@ -14,7 +14,7 @@
 SWEEPS = 2
 COUNT = MODES + 2
 HALF = COUNT // 2
-ZB = 48
+PIECES = 4
 F32 = jnp.float32
 BF16 = jnp.bfloat16
 HIGH = lax.Precision.HIGHEST
@@ -44,15 +44,16 @@
 def z_table(cz):
     taps = box_taps()
     boxes = cz // STRIDE
-    order = list(range(0, boxes, 2)) + list(range(1, boxes, 2)) + [-1, boxes]
-    table = np.zeros((3 * ZB, 2 * cz), np.float32)
+    deep = cz + 16
+    order = list(range(0, boxes, 2)) + list(range(1, boxes, 2))
+    table = np.zeros((3 * boxes, 2 * deep), np.float32)
     for block, which in enumerate((0, 1, 3)):
         for row, box in enumerate(order):
             for k in range(STRIDE + 4):
                 z = box * STRIDE - 2 + k
-                if 0 <= z < cz:
-                    table[block * ZB + row, z] = taps[which][k]
-                    table[block * ZB + row, cz + z] = taps[which][k]
+                at = cz + 10 + z if z < 0 else z
+                table[block * boxes + row, at] = taps[which][k]
+                table[block * boxes + row, deep + at] = taps[which][k]
     return table
 
 
@@ -116,6 +117,7 @@
     taps = box_taps()
     start = (jj - 1) * STRIDE - 2
     zc = 16
+    zb = z_ref.shape[0] // 3
 
     def body(i, carry):
         at = pl.multiple_of(i * zc, zc)
@@ -147,20 +149,20 @@
         return carry
 
     lax.fori_loop(0, cz // zc, body, 0)
-    z0 = z_ref[0:ZB, :]
+    z0 = z_ref[0:zb, :]
 
     def along_z(z, f):
         return jnp.dot(z, f_ref[:, f * ny : (f + 1) * ny], preferred_element_type=F32)
 
     z012_f0 = along_z(z_ref[...], 0)
-    z01_f1 = along_z(z_ref[0 : 2 * ZB, :], 1)
-    z01_f2 = along_z(z_ref[0 : 2 * ZB, :], 2)
+    z01_f1 = along_z(z_ref[0 : 2 * zb, :], 1)
+    z01_f2 = along_z(z_ref[0 : 2 * zb, :], 2)
     fields = [
-        z012_f0[0:ZB],
-        z01_f1[0:ZB] + z012_f0[ZB : 2 * ZB],
-        z01_f2[0:ZB],
-        along_z(z0, 3) + 2.0 * z01_f1[ZB : 2 * ZB] + z012_f0[2 * ZB : 3 * ZB],
-        along_z(z0, 4) + z01_f2[ZB : 2 * ZB],
+        z012_f0[0:zb],
+        z01_f1[0:zb] + z012_f0[zb : 2 * zb],
+        z01_f2[0:zb],
+        along_z(z0, 3) + 2.0 * z01_f1[zb : 2 * zb] + z012_f0[2 * zb : 3 * zb],
+        along_z(z0, 4) + z01_f2[zb : 2 * zb],
         along_z(z0, 5),
     ]
     out = None
@@ -169,7 +171,7 @@
         yh = yh_ref[k * ny : (k + 1) * ny, :]
         yl = yl_ref[k * ny : (k + 1) * ny, :]
         both = jnp.dot(jnp.concatenate([high, low], axis=0), yh, preferred_element_type=F32)
-        term = both[:ZB] + both[ZB:] + jnp.dot(high, yl, preferred_element_type=F32)
+        term = both[:zb] + both[zb:] + jnp.dot(high, yl, preferred_element_type=F32)
         out = term if out is None else out + term
     u_ref[jj, c, :, :] = out
 
@@ -229,7 +231,7 @@
     velocity_ref, basis_ref, levels_ref, index_ref, advect_ref, z_ref,
     out_ref, sigma_ref,
     v_ref, stack_ref, yh_ref, yl_ref, f_ref, u_ref, xr_ref, zs_ref, zr_ref, sn_ref, row_ref,
-    gram_ref, gm_ref, gs_ref,
+    gm_ref, gs_ref,
     v_sem, own_sem,
     s1_send, s1_recv, mate_send, mate_recv, s2_send, s2_recv, fb_send, fb_recv, fa_send, fa_recv,
     x_send, x_recv, z_send, z_recv, sn_send, sn_recv, gm_send, gm_recv, gs_send, gs_recv,
@@ -264,7 +266,9 @@
 
     v_copies = []
     for c in range(components):
-        copy = pltpu.make_async_copy(velocity_ref.at[c], v_ref.at[c], v_sem.at[c])
+        copy = pltpu.make_async_copy(
+            velocity_ref.at[c], v_ref.at[c, :, pl.ds(0, cz), :], v_sem.at[c]
+        )
         copy.start()
         v_copies.append(copy)
     own = pltpu.make_async_copy(basis_ref, stack_ref.at[rows_of(mode)], own_sem)
@@ -278,14 +282,33 @@
     pl.semaphore_wait(barrier, n_mode - 1 + n_space - 1)
 
     stage1 = []
-    for o in range(1, n_mode):
-        peer = mode_peer(o)
-        copy = remote(
-            basis_ref.at[:, cols_of(peer)], stack_ref.at[rows_of(mode), cols_of(peer)],
-            s1_send.at[o - 1], s1_recv.at[o - 1], space, peer,
-        )
-        copy.start()
-        stage1.append(copy)
+
+    def send1(first, count, slot):
+        for o in range(1, n_mode):
+            peer = mode_peer(o)
+            where = pl.ds(pl.multiple_of(peer * quarter + first, 128), count)
+            copy = remote(
+                basis_ref.at[:, where], stack_ref.at[rows_of(mode), where],
+                s1_send.at[slot, o - 1], s1_recv.at[slot, o - 1], space, peer,
+            )
+            copy.start()
+            stage1.append(copy)
+
+    eighth = quarter // 8
+    send1(0, eighth, 0)
+    for c in range(components):
+        v_copies[c].wait()
+        for x in range(cx):
+            row = (c * cx + x) * 2
+            zs_ref[0, row : row + 2, :] = v_ref[c, x, 0:2, :]
+            zs_ref[1, row : row + 2, :] = v_ref[c, x, cz - 2 : cz, :]
+    z_copies = [
+        remote(zs_ref.at[0], zr_ref.at[0], z_send.at[0], z_recv.at[0], space, mode_peer(n_mode - 1)),
+        remote(zs_ref.at[1], zr_ref.at[1], z_send.at[1], z_recv.at[1], space, mode_peer(1)),
+    ]
+    for copy in z_copies:
+        copy.start()
+    send1(eighth, quarter - eighth, 1)
     mates = []
     mate_cols = [cols_of(mode)] + [
         cols_of(2 * lax.rem(pair + g, pairs), 2) for g in range(1, pairs)
@@ -300,9 +323,14 @@
 
     wall_tables(levels_ref, index_ref, advect_ref, yh_ref, yl_ref)
     row_ref[...] = jnp.zeros_like(row_ref)
-    zs_ref[...] = jnp.zeros_like(zs_ref)
-    for copy in v_copies:
+    for copy in z_copies:
         copy.wait()
+    v_ref[:, :, cz : cz + 16, :] = jnp.zeros((components, cx, 16, ny), F32)
+    for c in range(components):
+        for x in range(cx):
+            row = (c * cx + x) * 2
+            for d in range(2):
+                v_ref[c, x, cz + 8 * d : cz + 8 * d + 2, :] = zr_ref[d, row : row + 2, :]
 
     def boxes(jj):
         def body(c, carry):
@@ -326,26 +354,11 @@
     for c in range(components):
         u_ref[nxb, c, :, :] = u_ref[nxb, c, :, :] + xr_ref[0, c, :, :]
         u_ref[1, c, :, :] = u_ref[1, c, :, :] + xr_ref[1, c, :, :]
-    for c in range(components):
-        for jj in range(1, nxb + 1):
-            row = c * nxb + jj - 1
-            for d in range(2):
-                zs_ref[d, row : row + 1, :] = u_ref[jj, c, nzb + d : nzb + d + 1, :]
-    z_copies = [
-        remote(zs_ref.at[0], zr_ref.at[0], z_send.at[0], z_recv.at[0], space, mode_peer(n_mode - 1)),
-        remote(zs_ref.at[1], zr_ref.at[1], z_send.at[1], z_recv.at[1], space, mode_peer(1)),
-    ]
-    for copy in z_copies:
-        copy.start()
-    for copy in z_copies:
-        copy.wait()
     half = nzb // 2
     lanes = lax.broadcasted_iota(jnp.int32, (half, 2 * nb), 1) < nb
     for c in range(components):
         for jj in range(1, nxb + 1):
             row = c * nxb + jj - 1
-            u_ref[jj, c, nzb - 1 : nzb, :] = u_ref[jj, c, nzb - 1 : nzb, :] + zr_ref[0, row : row + 1, :]
-            u_ref[jj, c, 0:1, :] = u_ref[jj, c, 0:1, :] + zr_ref[1, row : row + 1, :]
             even = u_ref[jj, c, 0:half, :]
             odd = u_ref[jj, c, half:nzb, :]
             one = jnp.where(lanes, even, pltpu.roll(odd, nb, 1))
@@ -357,14 +370,8 @@
                 lane_at = (at + k) * 2 * nb
                 row_ref[0:1, lane_at : lane_at + 2 * nb] = one[k : k + 1]
                 row_ref[1:2, lane_at : lane_at + 2 * nb] = two[k : k + 1]
-    sn_copies = []
-    for o in range(1, n_mode):
-        copy = remote(
-            sn_ref.at[mode], sn_ref.at[mode], sn_send.at[o - 1], sn_recv.at[o - 1],
-            space, mode_peer(o),
-        )
-        copy.start()
-        sn_copies.append(copy)
+    sn_mate = remote(sn_ref.at[mode], sn_ref.at[mode], sn_send.at[0], sn_recv.at[0], space, mate)
+    sn_mate.start()
 
     for copy in stage1:
         copy.wait()
@@ -376,22 +383,15 @@
         copy = remote(where, where, fb_send.at[g - 1], fb_recv.at[g - 1], space, mate)
         copy.start()
         forward_b.append(copy)
-    stage2 = []
+    sn_copies = []
     for g in range(1, pairs):
-        for k in range(1, pairs):
-            there = lax.rem(pair + g, pairs)
-            piece = lax.rem(there + k, pairs)
-            for part in range(2):
-                i = ((g - 1) * (pairs - 1) + k - 1) * 2 + part
-                where = cols_of(2 * piece + part)
-                copy = remote(
-                    basis_ref.at[:, where], stack_ref.at[rows_of(mode), where],
-                    s2_send.at[i], s2_recv.at[i], space, 2 * there + side,
-                )
-                copy.start()
-                source = lax.rem(pair - g + pairs, pairs)
-                here = lax.rem(pair + k, pairs)
-                stage2.append((copy, i, source, 2 * here + part))
+        copy = remote(
+            sn_ref.at[mode], sn_ref.at[mode], sn_send.at[g], sn_recv.at[g],
+            space, 2 * lax.rem(pair + g, pairs) + side,
+        )
+        copy.start()
+        source = 2 * lax.rem(pair - g + pairs, pairs) + side
+        sn_copies.append((copy, source, g))
 
     kc = 2048
 
@@ -422,6 +422,26 @@
         gm_copies.append(copy)
     for copy in gm_copies:
         copy.wait()
+    stage2 = []
+    piece_cols = quarter // PIECES
+    for part in range(2 * PIECES):
+        for g in range(1, pairs):
+            for k in range(1, pairs):
+                i = ((g - 1) * (pairs - 1) + k - 1) * 2 * PIECES + part
+                there = lax.rem(pair + g, pairs)
+
+                def piece(group):
+                    first = 2 * quarter * lax.rem(group, pairs) + part * piece_cols
+                    return pl.ds(pl.multiple_of(first, piece_cols), piece_cols)
+
+                where = piece(there + k)
+                copy = remote(
+                    basis_ref.at[:, where], stack_ref.at[rows_of(mode), where],
+                    s2_send.at[i], s2_recv.at[i], space, 2 * there + side,
+                )
+                copy.start()
+                source = 2 * lax.rem(pair - g + pairs, pairs) + side
+                stage2.append((copy, i, source, piece(pair + k), lax.rem(pair + k, pairs), part))
     total = gm_ref[0]
     for m in range(1, n_mode):
         total = total + gm_ref[m]
@@ -456,7 +476,7 @@
     norms = across(jnp.broadcast_to(norm_lead, (8, 128)), pick(0, 128, True)) + across(
         jnp.broadcast_to(norm_trail, (8, 128)), pick(0, 128, False)
     )
-    sigma_ref[...] = jnp.sqrt(norms)
+    sigma_ref[...] = jnp.sqrt(norms[0:1, 0:MODES])
     sel_lead, sel_trail = pick(mode * mb, mb, True), pick(mode * mb, mb, False)
     lead_b = jnp.concatenate([lead[8:], lead[8:]], axis=0)
     trail_b = jnp.concatenate([trail[8:], trail[8:]], axis=0)
@@ -467,15 +487,15 @@
     c0 = jnp.broadcast_to(snap[:, 0:1], (mb, 128))
     c1 = jnp.broadcast_to(snap[:, 1:2], (mb, 128))
 
-    def emit(q):
+    def emit(q, first, count):
         def body(i, carry):
-            at = pl.multiple_of(q * quarter + i * kc, kc)
+            at = pl.multiple_of(q * quarter + first + i * kc, kc)
             high, low = split(stack_ref[:, pl.ds(at, kc)])
             both = jnp.concatenate([high, low], axis=0)
             done = jnp.dot(left, both, preferred_element_type=F32)
             done = done[:mb] + done[mb:]
             for t in range(kc // 128):
-                r = i * (kc // 128) + t
+                r = first // 128 + i * (kc // 128) + t
                 out_ref[:, pl.ds(pl.multiple_of(at + t * 128, 128), 128)] = (
                     done[:, t * 128 : (t + 1) * 128]
                     + c0 * sn_ref[q, 0, pl.ds(r, 1), :]
@@ -483,26 +503,44 @@
                 )
             return carry
 
-        lax.fori_loop(0, quarter // kc, body, 0)
-
-    for copy in sn_copies + mates + forward_b:
+        lax.fori_loop(0, count // kc, body, 0)
+
+    for copy in mates + forward_b + [sn_mate]:
         copy.wait()
-    forward_a = []
-    emit(2 * pair)
-    for n, (copy, i, source, q) in enumerate(stage2):
+    sn_forward = []
+    for copy, source, g in sn_copies:
         copy.wait()
-        where = stack_ref.at[rows_of(2 * source + side), cols_of(q)]
-        forward = remote(where, where, fa_send.at[i], fa_recv.at[i], space, mate)
+        i = pairs + g - 1
+        forward = remote(sn_ref.at[source], sn_ref.at[source], sn_send.at[i], sn_recv.at[i], space, mate)
         forward.start()
-        forward_a.append(forward)
-        if n == 0:
-            emit(2 * pair + 1)
-    if not stage2:
-        emit(2 * pair + 1)
-    for copy in forward_a:
-        copy.wait()
-    for o in range(2, n_mode):
-        emit(lax.rem(2 * pair + o, n_mode))
+        sn_forward.append(forward)
+    emit(2 * pair, 0, quarter)
+    emit(2 * pair + 1, 0, quarter)
+    for forward in sn_forward:
+        forward.wait()
+    size = (pairs - 1) ** 2
+    before = []
+    for n in range(0, len(stage2), size or 1):
+        group = stage2[n : n + size]
+        forwards = []
+        for copy, i, source, where, _, _ in group:
+            copy.wait()
+            rows = stack_ref.at[rows_of(source), where]
+            forward = remote(rows, rows, fa_send.at[i], fa_recv.at[i], space, mate)
+            forward.start()
+            forwards.append(forward)
+        finish(before, emit, pairs, piece_cols)
+        before = list(zip(forwards, group))
+    finish(before, emit, pairs, piece_cols)
+
+
+def finish(before, emit, pairs, piece_cols):
+    for forward, _ in before:
+        forward.wait()
+    for _, (_, _, _, _, group, part) in before[: pairs - 1]:
+        first = part * piece_cols
+        quarter = PIECES * piece_cols
+        emit(2 * group + first // quarter, first % quarter, piece_cols)
 
 
 def per_device(n_space, n_mode, velocity, basis, levels, profile_index, advect):
@@ -511,13 +549,13 @@
     quarter = cols // n_mode
     nxb, nzb, nb = cx // STRIDE, cz // STRIDE, ny // STRIDE
     pairs = n_mode // 2
-    pieces = max(1, 2 * (pairs - 1) ** 2)
+    pieces = max(1, 2 * PIECES * (pairs - 1) ** 2)
     dma = pltpu.SemaphoreType.DMA
     modes, sigma = pl.pallas_call(
         functools.partial(kernel, n_space, n_mode),
         out_shape=(
             jax.ShapeDtypeStruct((mb, cols), F32),
-            jax.ShapeDtypeStruct((8, 128), F32),
+            jax.ShapeDtypeStruct((1, MODES), F32),
         ),
         in_specs=[
             pl.BlockSpec(memory_space=pl.ANY),
@@ -532,29 +570,28 @@
             pl.BlockSpec(memory_space=pltpu.VMEM),
         ),
         scratch_shapes=[
-            pltpu.VMEM((components, cx, cz, ny), F32),
+            pltpu.VMEM((components, cx, cz + 16, ny), F32),
             pltpu.VMEM((n_mode * mb, cols), F32),
             pltpu.VMEM((6 * ny, 2 * nb), BF16),
             pltpu.VMEM((6 * ny, 2 * nb), BF16),
-            pltpu.VMEM((2 * cz, 6 * ny), BF16),
-            pltpu.VMEM((nxb + 2, components, ZB, 2 * nb), F32),
-            pltpu.VMEM((2, components, ZB, 2 * nb), F32),
-            pltpu.VMEM((2, 16, 2 * nb), F32),
-            pltpu.VMEM((2, 16, 2 * nb), F32),
+            pltpu.VMEM((2 * cz + 32, 6 * ny), BF16),
+            pltpu.VMEM((nxb + 2, components, nzb, 2 * nb), F32),
+            pltpu.VMEM((2, components, nzb, 2 * nb), F32),
+            pltpu.VMEM((2, components * cx * 2, ny), F32),
+            pltpu.VMEM((2, components * cx * 2, ny), F32),
             pltpu.VMEM((n_mode, 2, components * nxb * nzb // 2, 2 * nb), F32),
             pltpu.VMEM((16, quarter), F32),
-            pltpu.VMEM((8, 128), F32),
             pltpu.VMEM((n_mode, 8 + n_mode * mb, 128), F32),
             pltpu.VMEM((n_space, 8 + n_mode * mb, 128), F32),
             dma((components,)), dma,
-            dma((n_mode - 1,)), dma((n_mode - 1,)),
+            dma((2, n_mode - 1)), dma((2, n_mode - 1)),
             dma((pairs,)), dma((pairs,)),
             dma((pieces,)), dma((pieces,)),
             dma((max(1, pairs - 1),)), dma((max(1, pairs - 1),)),
             dma((pieces,)), dma((pieces,)),
             dma((2,)), dma((2,)),
             dma((2,)), dma((2,)),
-            dma((n_mode - 1,)), dma((n_mode - 1,)),
+            dma((2 * pairs - 1,)), dma((2 * pairs - 1,)),
             dma((n_mode - 1,)), dma((n_mode - 1,)),
             dma((n_space - 1,)), dma((n_space - 1,)),
         ],
@@ -569,7 +606,7 @@
         advect.reshape(1, -1),
         jnp.asarray(z_table(cz), BF16),
     )
-    return modes, sigma[0, :MODES]
+    return modes, sigma.reshape(-1)
 
 
 def solution(mesh):

time: 119 us -> 95.5 us (0.80)
  Pallas kernels: 113 us -> 90.4 us
    pallas_call x1, Pallas kernels: 113 us -> 90.4 us  [per_device(): pl.pallas_call(functools.partial(kernel, n_space, n_mode), out_shape=(jax...]
    unnamed x1 -> x4, local copies, waits for them, and re-layouts: 3.75 us -> 4.27 us
where the time goes in v2:
time: 95.5 us; the launch traced here: 95.3 us
  Pallas kernels  90.4 us (95%)
  local copies, waits for them, and re-layouts  4.27 us (4%)
    pallas_call x1, Pallas kernels, per_device(): pl.pallas_call(functools.partial(kernel, n_space, n_mode), out_shape=(jax...  90.4 us
    unnamed x4, local copies, waits for them, and re-layouts  4.27 us

profile of v2, /device:TPU:0, one launch (start us, length us, event | category | flops | bytes accessed | tf_op | source)
XLA Modules:
  0.0 95.3 jit_solution(2459771817050368503)
XLA Ops:
  0.6 90.4 %shard_map.77 = (f32[8,98304]{1,0:T(8,128)}, f32[1,32]{1,0:T(1,128)}) custom-call(f32[3,16,128,256]{3,2,1,0:T(8,128)} %velocity_ref.1, f32[8,98304]{1,0:T(8,128)} %basis_ref.1, f32[8]{0:T(128)} %levels_ref.1, s32[1,256]{1,0:T(1,128)} %bitcast.3, f32[1,256]{1,0:T(1,128)} %bitcast.4, bf16[96,288]{1,0:T(8,128)(2,1)} %constant.2.clone.z_ref), custom_call_target="tpu_custom_call" | custom-call | tf_op jit(solution)/shard_map/pallas_call | solution.py:554
  91.0 0.0 copy-start
  91.0 3.8 %copy.10 = f32[8,98304]{1,0:T(8,128)} copy(f32[8,98304]{1,0:T(8,128)} %get-tuple-element.8) | data formatting | bytes 6291456
  94.8 0.0 copy-done
  94.8 0.5 copy.11
Async XLA Ops:
  91.0 3.8 %copy-start = (f32[1,32]{1,0:T(1,128)S(1)}, f32[1,32]{1,0:T(1,128)}, u32[]{:S(2)}) copy-start(f32[1,32]{1,0:T(1,128)} %get-tuple-element.5) | copy-start | bytes 388

commit v3 on v2

--- a/solution.py
+++ b/solution.py
@@ -229,10 +229,10 @@
 def kernel(
     n_space, n_mode,
     velocity_ref, basis_ref, levels_ref, index_ref, advect_ref, z_ref,
-    out_ref, sigma_ref,
-    v_ref, stack_ref, yh_ref, yl_ref, f_ref, u_ref, xr_ref, zs_ref, zr_ref, sn_ref, row_ref,
+    modes_ref, sigma_ref,
+    out_ref, v_ref, stack_ref, yh_ref, yl_ref, f_ref, u_ref, xr_ref, zs_ref, zr_ref, sn_ref, row_ref,
     gm_ref, gs_ref,
-    v_sem, own_sem,
+    v_sem, own_sem, out_sem,
     s1_send, s1_recv, mate_send, mate_recv, s2_send, s2_recv, fb_send, fb_recv, fa_send, fa_recv,
     x_send, x_recv, z_send, z_recv, sn_send, sn_recv, gm_send, gm_recv, gs_send, gs_recv,
 ):
@@ -372,6 +372,15 @@
                 row_ref[1:2, lane_at : lane_at + 2 * nb] = two[k : k + 1]
     sn_mate = remote(sn_ref.at[mode], sn_ref.at[mode], sn_send.at[0], sn_recv.at[0], space, mate)
     sn_mate.start()
+    sn_copies = []
+    for g in range(1, pairs):
+        copy = remote(
+            sn_ref.at[mode], sn_ref.at[mode], sn_send.at[g], sn_recv.at[g],
+            space, 2 * lax.rem(pair + g, pairs) + side,
+        )
+        copy.start()
+        source = 2 * lax.rem(pair - g + pairs, pairs) + side
+        sn_copies.append((copy, source, g))
 
     for copy in stage1:
         copy.wait()
@@ -383,16 +392,29 @@
         copy = remote(where, where, fb_send.at[g - 1], fb_recv.at[g - 1], space, mate)
         copy.start()
         forward_b.append(copy)
-    sn_copies = []
-    for g in range(1, pairs):
-        copy = remote(
-            sn_ref.at[mode], sn_ref.at[mode], sn_send.at[g], sn_recv.at[g],
-            space, 2 * lax.rem(pair + g, pairs) + side,
-        )
-        copy.start()
-        source = 2 * lax.rem(pair - g + pairs, pairs) + side
-        sn_copies.append((copy, source, g))
-
+    stage2 = []
+    piece_cols = quarter // PIECES
+
+    def send2(part):
+        for g in range(1, pairs):
+            for k in range(1, pairs):
+                i = ((g - 1) * (pairs - 1) + k - 1) * 2 * PIECES + part
+                there = lax.rem(pair + g, pairs)
+
+                def piece(group):
+                    first = 2 * quarter * lax.rem(group, pairs) + part * piece_cols
+                    return pl.ds(pl.multiple_of(first, piece_cols), piece_cols)
+
+                where = piece(there + k)
+                copy = remote(
+                    basis_ref.at[:, where], stack_ref.at[rows_of(mode), where],
+                    s2_send.at[i], s2_recv.at[i], space, 2 * there + side,
+                )
+                copy.start()
+                source = 2 * lax.rem(pair - g + pairs, pairs) + side
+                stage2.append((copy, i, source, piece(pair + k), lax.rem(pair + k, pairs), part))
+
+    send2(0)
     kc = 2048
 
     def gram_body(i, carry):
@@ -420,28 +442,11 @@
         )
         copy.start()
         gm_copies.append(copy)
+    send2(1)
     for copy in gm_copies:
         copy.wait()
-    stage2 = []
-    piece_cols = quarter // PIECES
-    for part in range(2 * PIECES):
-        for g in range(1, pairs):
-            for k in range(1, pairs):
-                i = ((g - 1) * (pairs - 1) + k - 1) * 2 * PIECES + part
-                there = lax.rem(pair + g, pairs)
-
-                def piece(group):
-                    first = 2 * quarter * lax.rem(group, pairs) + part * piece_cols
-                    return pl.ds(pl.multiple_of(first, piece_cols), piece_cols)
-
-                where = piece(there + k)
-                copy = remote(
-                    basis_ref.at[:, where], stack_ref.at[rows_of(mode), where],
-                    s2_send.at[i], s2_recv.at[i], space, 2 * there + side,
-                )
-                copy.start()
-                source = 2 * lax.rem(pair - g + pairs, pairs) + side
-                stage2.append((copy, i, source, piece(pair + k), lax.rem(pair + k, pairs), part))
+    for part in range(2, 2 * PIECES):
+        send2(part)
     total = gm_ref[0]
     for m in range(1, n_mode):
         total = total + gm_ref[m]
@@ -504,7 +509,14 @@
             return carry
 
         lax.fori_loop(0, count // kc, body, 0)
-
+        where = pl.ds(pl.multiple_of(q * quarter + first, kc), count)
+        copy = pltpu.make_async_copy(
+            out_ref.at[:, where], modes_ref.at[:, where], out_sem.at[len(stores)]
+        )
+        copy.start()
+        stores.append(copy)
+
+    stores = []
     for copy in mates + forward_b + [sn_mate]:
         copy.wait()
     sn_forward = []
@@ -532,6 +544,8 @@
         finish(before, emit, pairs, piece_cols)
         before = list(zip(forwards, group))
     finish(before, emit, pairs, piece_cols)
+    for copy in stores:
+        copy.wait()
 
 
 def finish(before, emit, pairs, piece_cols):
@@ -566,10 +580,11 @@
             pl.BlockSpec(memory_space=pltpu.VMEM),
         ],
         out_specs=(
-            pl.BlockSpec(memory_space=pltpu.VMEM),
+            pl.BlockSpec(memory_space=pl.ANY),
             pl.BlockSpec(memory_space=pltpu.VMEM),
         ),
         scratch_shapes=[
+            pltpu.VMEM((mb, cols), F32),
             pltpu.VMEM((components, cx, cz + 16, ny), F32),
             pltpu.VMEM((n_mode * mb, cols), F32),
             pltpu.VMEM((6 * ny, 2 * nb), BF16),
@@ -583,7 +598,7 @@
             pltpu.VMEM((16, quarter), F32),
             pltpu.VMEM((n_mode, 8 + n_mode * mb, 128), F32),
             pltpu.VMEM((n_space, 8 + n_mode * mb, 128), F32),
-            dma((components,)), dma,
+            dma((components,)), dma, dma((2 + 2 * PIECES * (pairs - 1),)),
             dma((2, n_mode - 1)), dma((2, n_mode - 1)),
             dma((pairs,)), dma((pairs,)),
             dma((pieces,)), dma((pieces,)),
@@ -606,7 +621,37 @@
         advect.reshape(1, -1),
         jnp.asarray(z_table(cz), BF16),
     )
+    modes, sigma = pl.pallas_call(
+        hand_over,
+        out_shape=(
+            jax.ShapeDtypeStruct((mb, cols), F32),
+            jax.ShapeDtypeStruct((1, MODES), F32),
+        ),
+        in_specs=[pl.BlockSpec(memory_space=pl.ANY), pl.BlockSpec(memory_space=pltpu.VMEM)],
+        out_specs=(
+            pl.BlockSpec(memory_space=pl.ANY),
+            pl.BlockSpec(memory_space=pltpu.VMEM),
+        ),
+        scratch_shapes=[pltpu.VMEM((mb, cols), F32), dma((8,)), dma((8,))],
+        compiler_params=pltpu.CompilerParams(vmem_limit_bytes=60 * 1024 * 1024),
+    )(modes, sigma)
     return modes, sigma.reshape(-1)
+
+
+def hand_over(modes_ref, sigma_ref, out_ref, sigma_out_ref, held_ref, in_sem, out_sem):
+    width = modes_ref.shape[1] // 8
+    loads, stores = [], []
+    for i in range(8):
+        part = (slice(None), pl.ds(i * width, width))
+        loads.append(pltpu.make_async_copy(modes_ref.at[part], held_ref.at[part], in_sem.at[i]))
+        stores.append(pltpu.make_async_copy(held_ref.at[part], out_ref.at[part], out_sem.at[i]))
+        loads[i].start()
+    sigma_out_ref[...] = sigma_ref[...]
+    for load, store in zip(loads, stores):
+        load.wait()
+        store.start()
+    for store in stores:
+        store.wait()
 
 
 def solution(mesh):

time: 95.5 us -> 92.2 us (0.965)
  local copies, waits for them, and re-layouts: 4.27 us -> 0 us
  Pallas kernels: 90.4 us -> 91.4 us
    unnamed x4 -> x0, local copies, waits for them, and re-layouts: 4.27 us -> none
    pallas_call x0 -> x1, Pallas kernels: none -> 3.98 us  [per_device(): pl.pallas_call(hand_over, out_shape=(jax.ShapeDtypeStruct((mb, cols), F32...]
    pallas_call x1, Pallas kernels: 90.4 us -> 87.4 us  [per_device(): pl.pallas_call(functools.partial(kernel, n_space, n_mode), out_shape=(jax...]
where the time goes in v3:
time: 92.2 us; the launch traced here: 92 us
  Pallas kernels  91.4 us (99%)
    pallas_call x1, Pallas kernels, per_device(): pl.pallas_call(functools.partial(kernel, n_space, n_mode), out_shape=(jax...  87.4 us
    pallas_call x1, Pallas kernels, per_device(): pl.pallas_call(hand_over, out_shape=(jax.ShapeDtypeStruct((mb, cols), F32...  3.98 us

profile of v3, /device:TPU:0, one launch (start us, length us, event | category | flops | bytes accessed | tf_op | source)
XLA Modules:
  0.0 92.0 jit_solution(136410271725313900)
XLA Ops:
  0.6 87.4 %shard_map.77 = (f32[8,98304]{1,0:T(8,128)}, f32[1,32]{1,0:T(1,128)}) custom-call(f32[3,16,128,256]{3,2,1,0:T(8,128)} %velocity_ref.1, f32[8,98304]{1,0:T(8,128)} %basis_ref.1, f32[8]{0:T(128)} %levels_ref.1, s32[1,256]{1,0:T(1,128)} %bitcast.3, f32[1,256]{1,0:T(1,128)} %bitcast.4, bf16[96,288]{1,0:T(8,128)(2,1)} %constant.2.clone.z_ref), custom_call_target="tpu_custom_call" | custom-call | tf_op jit(solution)/shard_map/pallas_call | solution.py:568
  88.1 4.0 %shard_map.78 = (f32[8,98304]{1,0:T(8,128)}, f32[1,32]{1,0:T(1,128)}) custom-call(f32[8,98304]{1,0:T(8,128)} %get-tuple-element.6.modes_ref, f32[1,32]{1,0:T(1,128)} %get-tuple-element.7.sigma_ref), custom_call_target="tpu_custom_call" | custom-call | tf_op jit(solution)/shard_map/pallas_call | solution.py:624
